TPU v7x, 512 devices: a whole 4x8x8 slice. The times are simulated.
512 devices in a mesh: grp: 16 (over x, z_hi), body: 32 (over y, z_lo, core).
Axes of the slice: x: 4, y: 8, z: 8 (z_hi: 4, z_lo: 2; z = z_hi * 2 + z_lo), core: 2. Of those that a mesh axis runs over, the one named last changes fastest.
Arguments:
- incident: bfloat16 [512, 16, 512], P(('grp', 'body')), may hold values from -6 to 6
- exciting: float32 [512, 16, 512], P(('grp', 'body')), may hold values from -6 to 6
- t_matrices: bfloat16 [512, 2, 256, 256], P(('grp', 'body')), may hold values from -0.1875 to 0.1875
- hankel_rows: bfloat16 [225, 2, 512], replicated, may hold values from -0.046875 to 0.046875
- offsets: int32 [512, 32], P(('grp', 'body')), may hold values from 0 to 224
- lattice_slots: int32 [512], P('grp'), may hold values from 0 to 31, as said below
- up_maps: bfloat16 [512, 2, 256, 512], P(('grp', 'body')), may hold values from -0.0625 to 0.0625
- down_maps: bfloat16 [512, 2, 512, 256], P(('grp', 'body')), may hold values from -0.1875 to 0.1875
- group_maps: bfloat16 [16, 16, 2, 512, 512], P('grp', None, None, 'body'), may hold values from -0.046875 to 0.046875
Outputs:
- updated: float32 [512, 16, 512], P(('grp', 'body'))
Inputs may be any that keep to these rules, and one draw needn't show every extreme that they name: `lattice_slots`: within each group the 32 columns stand at the slots 0 to 31, one column a slot.
All inputs are finite; a program needn't handle non-finite values.
Results may differ from a plain program's by a relative error of at most 0.0034.
Values may be sent and summed in bfloat16 or wider, within the bound.
A program may use at most 64 MiB of HBM per device.

v0:
```python
import math
import jax
import jax.numpy as jnp
from jax import lax
from jax.sharding import PartitionSpec as P


def complex_apply(form, values, real_mats, imag_mats):
    half_width = values.shape[-1] // 2
    real_values = values[..., :half_width]
    imag_values = values[..., half_width:]
    real_out = jnp.einsum(
        form, real_values, real_mats, preferred_element_type=jnp.float32
    ) - jnp.einsum(form, imag_values, imag_mats, preferred_element_type=jnp.float32)
    imag_out = jnp.einsum(
        form, real_values, imag_mats, preferred_element_type=jnp.float32
    ) + jnp.einsum(form, imag_values, real_mats, preferred_element_type=jnp.float32)
    return jnp.concatenate([real_out, imag_out], axis=-1)


def toeplitz_mats(sequences):
    length = sequences.shape[-1] // 2
    repeats = (1,) * (sequences.ndim - 1) + (length,)
    tiled = jnp.tile(sequences, repeats)
    window = tiled[..., length : length + length * (2 * length - 1)]
    return window.reshape(sequences.shape[:-1] + (length, 2 * length - 1))[..., :length]


def local(
    incident,
    exciting,
    t_matrices,
    hankel_rows,
    offsets,
    lattice_slots,
    up_maps,
    down_maps,
    group_maps,
):
    body_index = lax.axis_index("body")
    group_index = lax.axis_index("grp")
    local_count = incident.shape[0]
    scattered = complex_apply("iln,inm->ilm", incident, t_matrices[:, 0], t_matrices[:, 1]).astype(
        jnp.bfloat16
    )
    own_members = body_index * local_count + jnp.arange(local_count, dtype=jnp.int32)
    zero_seq = jnp.zeros((), jnp.bfloat16)
    all_offsets = lax.all_gather(offsets, "body", axis=0, tiled=True)
    group_count = lattice_slots.shape[0]
    own_slots = lax.dynamic_slice_in_dim(lattice_slots, body_index * local_count, local_count, 0)
    table_rows = jnp.take(all_offsets, own_slots, axis=1)
    sequences = jnp.take(hankel_rows, table_rows, axis=0)
    targets = jnp.arange(group_count, dtype=jnp.int32)
    keep = targets[:, None] != own_members[None, :]
    sequences = jnp.where(keep[:, :, None, None], sequences, zero_seq)
    block_rows = math.gcd(group_count, 4)
    sequences = sequences.reshape((group_count // block_rows, block_rows) + sequences.shape[1:])

    def one_block(block_seqs):
        mats = toeplitz_mats(block_seqs)
        return complex_apply("sln,tsnm->tlm", scattered, mats[:, :, 0], mats[:, :, 1])

    terms = lax.map(one_block, sequences)
    totals = lax.psum(terms.reshape((group_count,) + terms.shape[2:]), "body")
    near = lax.dynamic_slice_in_dim(totals, body_index * local_count, local_count, 0)
    partial_value = complex_apply("iln,inq->lq", scattered, up_maps[:, 0], up_maps[:, 1])
    expansion = lax.psum(partial_value, "body").astype(jnp.bfloat16)
    block_width = group_maps.shape[3]
    full_width = group_maps.shape[4]
    real_block = lax.dynamic_slice_in_dim(expansion, body_index * block_width, block_width, 1)
    imag_block = lax.dynamic_slice_in_dim(
        expansion, full_width + body_index * block_width, block_width, 1
    )
    own_block = jnp.concatenate([real_block, imag_block], axis=-1)[None]
    piece = lax.all_gather(own_block, "grp", axis=0, tiled=True)
    width = piece.shape[0]
    sources = jnp.arange(width, dtype=jnp.int32)
    piece = jnp.where((sources != group_index)[:, None, None], piece, zero_seq)
    mats = group_maps[0]
    incoming_part = complex_apply("hln,hnq->lq", piece, mats[:, 0], mats[:, 1])
    incoming = lax.psum(incoming_part, "body").astype(jnp.bfloat16)
    far = complex_apply("lq,iqp->ilp", incoming, down_maps[:, 0], down_maps[:, 1])
    return exciting + near + far


def solution(mesh):
    return jax.shard_map(
        local,
        mesh=mesh,
        in_specs=(
            P(("grp", "body"), None, None),
            P(("grp", "body"), None, None),
            P(("grp", "body"), None, None, None),
            P(),
            P(("grp", "body"), None),
            P("grp"),
            P(("grp", "body"), None, None, None),
            P(("grp", "body"), None, None, None),
            P("grp", None, None, "body", None),
        ),
        out_specs=P(("grp", "body"), None, None),
        check_vma=False,
    )
```

profile of v0, /device:TPU:32, one launch (start us, length us, event | category | flops | bytes accessed | tf_op | source)
XLA Modules:
  0.0 437.4 jit_solution(12570242964982283185)
XLA Ops:
  6.5 1.1 fusion.43
  7.7 1.1 fusion.39
  8.7 1.3 dynamic_slice.16
  12.1 32.7 %all-gather.1 = s32[32,1,32]{2,1,0:T(1,128)S(1)} all-gather(s32[1,1,32]{2,1,0:T(1,128)} %bitcast.159), channel_id=1, replica_groups=mesh['grp'=16,'body'=32] {'body'}, dimensions={0}, use_global_device_ids=true | all-gather | bytes 4224 | tf_op jit(solution)/shard_map/all_gather | solution.py:48
  44.8 1.3 fusion.67
  46.2 1.1 fusion.17
  47.3 1.1 fusion.18
  48.4 0.7 gather_fusion
  49.3 119.1 %while.11 = (s32[]{:T(128)}, f32[8,4,16,512]{3,2,1,0:T(8,128)}, bf16[8,4,1,2,512]{4,3,1,2,0:T(2,128)(2,1)S(1)}, bf16[1,16,512]{2,1,0:T(8,128)(2,1)S(1)}, s32[]{:T(128)}) while((s32[]{:T(128)}, f32[8,4,16,512]{3,2,1,0:T(8,128)}, bf16[8,4,1,2,512]{4,3,1,2,0:T(2,128)(2,1)S(1)}, bf16[1,16,512]{2,1,0:T(8,128)(2,1)S(1)}, s32[]{:T(128)}) %tuple.28), condition=%wide.region_1.2_spmd, body=%wide.region_0.1_spmd.sunk | while | flops 33619968 | bytes 17474112 | solution.py:63
  49.5 2.8 tile.14
  52.3 4.4 %slice.219 = bf16[4,1,2,130816]{3,2,0,1:T(2,128)(2,1)} slice(bf16[4,1,2,131072]{3,2,0,1:T(2,128)(2,1)} %tile.14), slice={[0:4], [0:1], [0:2], [256:131072]} | slice | bytes 4186112 | tf_op jit(solution)/shard_map/while/body/eval_jaxpr/slice | solution.py:25
  56.7 6.1 %reshape.288 = bf16[4,1,2,256,511]{4,3,2,0,1:T(8,128)(2,1)S(1)} reshape(bf16[4,1,2,130816]{3,2,0,1:T(2,128)(2,1)} %slice.219) | data formatting | bytes 4186112 | tf_op jit(solution)/shard_map/while/body/eval_jaxpr/reshape | solution.py:26
  63.0 0.2 fusion.88
  63.3 0.2 fusion.86
  63.5 0.7 fusion.89
  64.4 2.8 tile.14
  67.2 4.4 %slice.219 = bf16[4,1,2,130816]{3,2,0,1:T(2,128)(2,1)} slice(bf16[4,1,2,131072]{3,2,0,1:T(2,128)(2,1)} %tile.14), slice={[0:4], [0:1], [0:2], [256:131072]} | slice | bytes 4186112 | tf_op jit(solution)/shard_map/while/body/eval_jaxpr/slice | solution.py:25
  71.6 6.1 %reshape.288 = bf16[4,1,2,256,511]{4,3,2,0,1:T(8,128)(2,1)S(1)} reshape(bf16[4,1,2,130816]{3,2,0,1:T(2,128)(2,1)} %slice.219) | data formatting | bytes 4186112 | tf_op jit(solution)/shard_map/while/body/eval_jaxpr/reshape | solution.py:26
  77.8 0.2 fusion.88
  78.2 0.2 fusion.86
  78.4 0.7 fusion.89
  79.2 2.8 tile.14
  82.0 4.4 %slice.219 = bf16[4,1,2,130816]{3,2,0,1:T(2,128)(2,1)} slice(bf16[4,1,2,131072]{3,2,0,1:T(2,128)(2,1)} %tile.14), slice={[0:4], [0:1], [0:2], [256:131072]} | slice | bytes 4186112 | tf_op jit(solution)/shard_map/while/body/eval_jaxpr/slice | solution.py:25
  86.4 6.1 %reshape.288 = bf16[4,1,2,256,511]{4,3,2,0,1:T(8,128)(2,1)S(1)} reshape(bf16[4,1,2,130816]{3,2,0,1:T(2,128)(2,1)} %slice.219) | data formatting | bytes 4186112 | tf_op jit(solution)/shard_map/while/body/eval_jaxpr/reshape | solution.py:26
  92.7 0.2 fusion.88
  93.1 0.2 fusion.86
  93.3 0.7 fusion.89
  94.1 2.8 tile.14
  96.9 4.4 %slice.219 = bf16[4,1,2,130816]{3,2,0,1:T(2,128)(2,1)} slice(bf16[4,1,2,131072]{3,2,0,1:T(2,128)(2,1)} %tile.14), slice={[0:4], [0:1], [0:2], [256:131072]} | slice | bytes 4186112 | tf_op jit(solution)/shard_map/while/body/eval_jaxpr/slice | solution.py:25
  101.3 6.1 %reshape.288 = bf16[4,1,2,256,511]{4,3,2,0,1:T(8,128)(2,1)S(1)} reshape(bf16[4,1,2,130816]{3,2,0,1:T(2,128)(2,1)} %slice.219) | data formatting | bytes 4186112 | tf_op jit(solution)/shard_map/while/body/eval_jaxpr/reshape | solution.py:26
  107.6 0.2 fusion.88
  108.0 0.2 fusion.86
  108.2 0.7 fusion.89
  109.0 2.8 tile.14
  111.8 4.4 %slice.219 = bf16[4,1,2,130816]{3,2,0,1:T(2,128)(2,1)} slice(bf16[4,1,2,131072]{3,2,0,1:T(2,128)(2,1)} %tile.14), slice={[0:4], [0:1], [0:2], [256:131072]} | slice | bytes 4186112 | tf_op jit(solution)/shard_map/while/body/eval_jaxpr/slice | solution.py:25
  116.2 6.1 %reshape.288 = bf16[4,1,2,256,511]{4,3,2,0,1:T(8,128)(2,1)S(1)} reshape(bf16[4,1,2,130816]{3,2,0,1:T(2,128)(2,1)} %slice.219) | data formatting | bytes 4186112 | tf_op jit(solution)/shard_map/while/body/eval_jaxpr/reshape | solution.py:26
  122.5 0.2 fusion.88
  122.9 0.2 fusion.86
  123.0 0.7 fusion.89
  123.9 2.8 tile.14
  126.7 4.4 %slice.219 = bf16[4,1,2,130816]{3,2,0,1:T(2,128)(2,1)} slice(bf16[4,1,2,131072]{3,2,0,1:T(2,128)(2,1)} %tile.14), slice={[0:4], [0:1], [0:2], [256:131072]} | slice | bytes 4186112 | tf_op jit(solution)/shard_map/while/body/eval_jaxpr/slice | solution.py:25
  131.1 6.1 %reshape.288 = bf16[4,1,2,256,511]{4,3,2,0,1:T(8,128)(2,1)S(1)} reshape(bf16[4,1,2,130816]{3,2,0,1:T(2,128)(2,1)} %slice.219) | data formatting | bytes 4186112 | tf_op jit(solution)/shard_map/while/body/eval_jaxpr/reshape | solution.py:26
  137.4 0.2 fusion.88
  137.7 0.2 fusion.86
  137.9 0.7 fusion.89
  138.8 2.8 tile.14
  141.6 4.4 %slice.219 = bf16[4,1,2,130816]{3,2,0,1:T(2,128)(2,1)} slice(bf16[4,1,2,131072]{3,2,0,1:T(2,128)(2,1)} %tile.14), slice={[0:4], [0:1], [0:2], [256:131072]} | slice | bytes 4186112 | tf_op jit(solution)/shard_map/while/body/eval_jaxpr/slice | solution.py:25
  146.0 6.1 %reshape.288 = bf16[4,1,2,256,511]{4,3,2,0,1:T(8,128)(2,1)S(1)} reshape(bf16[4,1,2,130816]{3,2,0,1:T(2,128)(2,1)} %slice.219) | data formatting | bytes 4186112 | tf_op jit(solution)/shard_map/while/body/eval_jaxpr/reshape | solution.py:26
  152.2 0.2 fusion.88
  152.6 0.2 fusion.86
  152.8 0.7 fusion.89
  153.6 2.8 tile.14
  156.4 4.4 %slice.219 = bf16[4,1,2,130816]{3,2,0,1:T(2,128)(2,1)} slice(bf16[4,1,2,131072]{3,2,0,1:T(2,128)(2,1)} %tile.14), slice={[0:4], [0:1], [0:2], [256:131072]} | slice | bytes 4186112 | tf_op jit(solution)/shard_map/while/body/eval_jaxpr/slice | solution.py:25
  160.8 6.1 %reshape.288 = bf16[4,1,2,256,511]{4,3,2,0,1:T(8,128)(2,1)S(1)} reshape(bf16[4,1,2,130816]{3,2,0,1:T(2,128)(2,1)} %slice.219) | data formatting | bytes 4186112 | tf_op jit(solution)/shard_map/while/body/eval_jaxpr/reshape | solution.py:26
  167.5 0.2 fusion.86
  167.7 0.7 fusion.89
  169.0 104.8 %psum.22 = bf16[16,1024]{1,0:T(8,128)(2,1)S(1)} all-reduce(f32[16,1024]{1,0:T(8,128)S(1)} %pad_maximum_fusion), channel_id=1, replica_groups=mesh['grp'=16,'body'=32] {'body'}, use_global_device_ids=true, to_apply=%region_3.4 | all-reduce | flops 16384 | bytes 98304 | tf_op jit(solution)/shard_map/psum | solution.py:67
  274.0 48.7 %all-gather = bf16[256,32]{1,0:T(8,128)(2,1)S(1)} all-gather(bf16[16,32]{1,0:T(8,128)(2,1)S(1)} %pad_maximum_fusion.3), channel_id=2, replica_groups=mesh['grp'=16,'body'=32] {'grp'}, dimensions={0}, use_global_device_ids=true | all-gather | bytes 17408 | tf_op jit(solution)/shard_map/all_gather | solution.py:75
  322.9 0.3 convolution_bitcast_fusion.2
  323.2 0.3 convolution_bitcast_fusion
  323.5 0.2 fusion.13
  323.8 0.2 fusion.14
  324.0 104.5 %psum.23 = bf16[16,1024]{1,0:T(8,128)(2,1)S(1)} all-reduce(f32[16,1024]{1,0:T(8,128)S(1)} %pad_maximum_fusion.1), channel_id=1, replica_groups=mesh['grp'=16,'body'=32] {'body'}, use_global_device_ids=true, to_apply=%region_4.5 | all-reduce | flops 16384 | bytes 98304 | tf_op jit(solution)/shard_map/psum | solution.py:81
  429.2 1.4 maximum_add_fusion
  (67 shorter events, 6.2 us)
Async XLA Ops:
  6.5 41.9 %copy-start = (bf16[225,2,512]{2,1,0:T(2,128)(2,1)S(1)}, bf16[225,2,512]{2,1,0:T(2,128)(2,1)}, u32[]{:S(2)}) copy-start(bf16[225,2,512]{2,1,0:T(2,128)(2,1)} %param.14) | copy-start | bytes 1382404
  6.5 422.6 %all-reduce.2.cloned.1.call-start = ((), (), s32[]{:S(2)}) async-start(), calls=%async_computation | async-start | bytes 2097152 | tf_op jit(solution)/shard_map/psum | solution.py:64
  49.3 119.1 %copy-start.2 = (bf16[1,2,256,512]{3,2,1,0:T(8,128)(2,1)S(1)}, bf16[1,2,256,512]{3,2,1,0:T(8,128)(2,1)}, u32[]{:S(2)}) copy-start(bf16[1,2,256,512]{3,2,1,0:T(8,128)(2,1)} %param.17) | copy-start | bytes 1572868
  168.4 154.4 %copy-start.3 = (bf16[1,16,2,16,512]{4,3,2,1,0:T(8,128)(2,1)S(1)}, bf16[1,16,2,16,512]{4,3,2,1,0:T(8,128)(2,1)}, u32[]{:S(2)}) copy-start(bf16[1,16,2,16,512]{4,3,2,1,0:T(8,128)(2,1)} %param.19) | copy-start | bytes 1572868
  168.7 259.9 %copy-start.1 = (bf16[1,2,512,256]{3,2,1,0:T(8,128)(2,1)S(1)}, bf16[1,2,512,256]{3,2,1,0:T(8,128)(2,1)}, u32[]{:S(2)}) copy-start(bf16[1,2,512,256]{3,2,1,0:T(8,128)(2,1)} %param.18) | copy-start | bytes 1572868
  322.7 106.4 %copy-start.4 = (f32[1,16,512]{2,1,0:T(8,128)S(1)}, f32[1,16,512]{2,1,0:T(8,128)}, u32[]{:S(2)}) copy-start(f32[1,16,512]{2,1,0:T(8,128)} %param.12) | copy-start | bytes 98308
Sparse Core Ops, SparseCore 0:
  168.5 234.8 all-reduce.1
where the time goes:
time: 438 us; the launch traced here: 437 us
  blocking collectives  291 us (66%)
  local copies, waits for them, and re-layouts  110 us (25%)
  between operations  15.6 us (4%)
  matrix products  12.5 us (3%)
  other arithmetic  8.4 us (2%)
    psum x1, blocking collectives, local(): expansion = lax.psum(partial_value, 'body').astype(jnp.bfloat16)  105 us
    psum x1, blocking collectives, local(): incoming = lax.psum(incoming_part, 'body').astype(jnp.bfloat16)  105 us
    all_gather x1, blocking collectives, local(): piece = lax.all_gather(own_block, 'grp', axis=0, tiled=True)  48.7 us
    reshape x8, local copies, waits for them, and re-layouts, toeplitz_mats(): window.reshape(sequences.shape[:-1] + (length, 2 * length - 1))  48.7 us
    slice x8, local copies, waits for them, and re-layouts, toeplitz_mats(): window = tiled[..., length:length + length * (2 * length - 1)]  35.2 us
    all_gather x1, blocking collectives, local(): all_offsets = lax.all_gather(offsets, 'body', axis=0, tiled=True)  32.7 us
    another operation x24, local copies, waits for them, and re-layouts, toeplitz_mats(): tiled = jnp.tile(sequences, repeats)  23.8 us
  transfers between devices with their start and end apart: 1, of which 0 were waited for; matrix products, arithmetic and copies ran while one was open for 1% of the time, Pallas kernels for 0%

commit v1 on v0

--- a/solution.py
+++ b/solution.py
@@ -45,7 +45,10 @@
     )
     own_members = body_index * local_count + jnp.arange(local_count, dtype=jnp.int32)
     zero_seq = jnp.zeros((), jnp.bfloat16)
-    all_offsets = lax.all_gather(offsets, "body", axis=0, tiled=True)
+    frame_out = lax.axis_size("body")
+    reply = jnp.stack(frame_out * [offsets], axis=0)
+    back = lax.all_to_all(reply, axis_name="body", split_axis=0, concat_axis=0)
+    all_offsets = jnp.concatenate(back, axis=0)
     group_count = lattice_slots.shape[0]
     own_slots = lax.dynamic_slice_in_dim(lattice_slots, body_index * local_count, local_count, 0)
     table_rows = jnp.take(all_offsets, own_slots, axis=1)

time: 438 us -> 541 us (1.24)
  the two profiles are of different devices: /device:TPU:32 before, /device:TPU:1 now
where the time goes in v1:
time: 541 us; the launch traced here: 540 us
  blocking collectives  257 us (48%)
  waiting for transfers between devices  121 us (22%)
  local copies, waits for them, and re-layouts  110 us (20%)
  matrix products  17.2 us (3%)
  between operations  15.4 us (3%)
  starting transfers between devices  10.6 us (2%)
  other arithmetic  8.46 us (2%)
    psum x1, waiting for transfers between devices, local(): totals = lax.psum(terms.reshape((group_count,) + terms.shape[2:]), 'body')  121 us
    psum x1, blocking collectives, local(): incoming = lax.psum(incoming_part, 'body').astype(jnp.bfloat16)  112 us
    psum x1, blocking collectives, local(): expansion = lax.psum(partial_value, 'body').astype(jnp.bfloat16)  104 us
    reshape x8, local copies, waits for them, and re-layouts, toeplitz_mats(): window.reshape(sequences.shape[:-1] + (length, 2 * length - 1))  48.7 us
    all_gather x1, blocking collectives, local(): piece = lax.all_gather(own_block, 'grp', axis=0, tiled=True)  41.5 us
    slice x8, local copies, waits for them, and re-layouts, toeplitz_mats(): window = tiled[..., length:length + length * (2 * length - 1)]  34.6 us
    another operation x24, local copies, waits for them, and re-layouts, toeplitz_mats(): tiled = jnp.tile(sequences, repeats)  23.7 us
  transfers between devices with their start and end apart: 2, of which 1 were waited for; matrix products, arithmetic and copies ran while one was open for 2% of the time, Pallas kernels for 0%

profile of v1, /device:TPU:1, one launch (start us, length us, event | category | flops | bytes accessed | tf_op | source)
XLA Modules:
  0.0 539.6 jit_solution(1764532134577253470)
XLA Ops:
  6.5 1.4 stack.2
  7.9 10.6 %all-to-all-start = ((s32[32,1,32]{2,1,0:T(1,128)}), s32[32,1,32]{2,1,0:T(1,128)S(1)}, u32[]{:S(2)}, u32[]{:S(2)}) async-start(s32[32,1,32]{2,1,0:T(1,128)} %stack.2), calls=%async_computation | async-start | bytes 32768 | tf_op jit(solution)/shard_map/all_to_all | solution.py:50
  18.5 1.1 fusion.43
  19.6 1.1 fusion.39
  20.7 1.1 fusion.17
  21.7 1.1 fusion.25
  22.8 1.1 fusion.29
  23.9 1.1 fusion.18
  25.0 1.1 convolution_add_fusion.1
  26.1 1.1 convolution_subtract_fusion.1
  27.2 103.9 %psum.22 = bf16[16,1024]{1,0:T(8,128)(2,1)S(1)} all-reduce(f32[16,1024]{1,0:T(8,128)S(1)} %pad_maximum_fusion), channel_id=1, replica_groups=mesh['grp'=16,'body'=32] {'body'}, use_global_device_ids=true, to_apply=%region_3.4 | all-reduce | flops 16384 | bytes 98304 | tf_op jit(solution)/shard_map/psum | solution.py:70
  131.3 41.5 %all-gather = bf16[256,32]{1,0:T(8,128)(2,1)S(1)} all-gather(bf16[16,32]{1,0:T(8,128)(2,1)S(1)} %pad_maximum_fusion.3), channel_id=2, replica_groups=mesh['grp'=16,'body'=32] {'grp'}, dimensions={0}, use_global_device_ids=true | all-gather | bytes 17408 | tf_op jit(solution)/shard_map/all_gather | solution.py:78
  173.0 0.3 convolution_bitcast_fusion.2
  173.3 0.3 convolution_bitcast_fusion
  173.6 0.2 fusion.13
  173.9 0.6 dynamic_slice.16
  176.4 1.3 fusion.67
  177.8 0.7 gather_fusion
  178.7 118.5 %while.11 = (s32[]{:T(128)}, f32[8,4,16,512]{3,2,1,0:T(8,128)}, bf16[8,4,1,2,512]{4,3,1,2,0:T(2,128)(2,1)S(1)}, bf16[1,16,512]{2,1,0:T(8,128)(2,1)S(1)}, s32[]{:T(128)}) while((s32[]{:T(128)}, f32[8,4,16,512]{3,2,1,0:T(8,128)}, bf16[8,4,1,2,512]{4,3,1,2,0:T(2,128)(2,1)S(1)}, bf16[1,16,512]{2,1,0:T(8,128)(2,1)S(1)}, s32[]{:T(128)}) %tuple.29), condition=%wide.region_1.2_spmd, body=%wide.region_0.1_spmd.sunk | while | flops 33619968 | bytes 17474112 | solution.py:66
  178.9 2.8 tile.14
  181.7 4.3 slice.219
  186.0 6.1 %reshape.289 = bf16[4,1,2,256,511]{4,3,2,0,1:T(8,128)(2,1)S(1)} reshape(bf16[4,1,2,130816]{3,2,0,1:T(2,128)(2,1)} %slice.219) | data formatting | bytes 4186112 | tf_op jit(solution)/shard_map/while/body/eval_jaxpr/reshape | solution.py:26
  192.3 0.2 fusion.88
  192.7 0.2 fusion.86
  192.9 0.7 fusion.89
  193.7 2.8 tile.14
  196.5 4.3 slice.219
  200.8 6.1 %reshape.289 = bf16[4,1,2,256,511]{4,3,2,0,1:T(8,128)(2,1)S(1)} reshape(bf16[4,1,2,130816]{3,2,0,1:T(2,128)(2,1)} %slice.219) | data formatting | bytes 4186112 | tf_op jit(solution)/shard_map/while/body/eval_jaxpr/reshape | solution.py:26
  207.1 0.2 fusion.88
  207.7 0.7 fusion.89
  208.5 2.8 tile.14
  211.3 4.3 slice.219
  215.6 6.1 %reshape.289 = bf16[4,1,2,256,511]{4,3,2,0,1:T(8,128)(2,1)S(1)} reshape(bf16[4,1,2,130816]{3,2,0,1:T(2,128)(2,1)} %slice.219) | data formatting | bytes 4186112 | tf_op jit(solution)/shard_map/while/body/eval_jaxpr/reshape | solution.py:26
  222.5 0.7 fusion.89
  223.3 2.8 tile.14
  226.1 4.3 slice.219
  230.5 6.1 %reshape.289 = bf16[4,1,2,256,511]{4,3,2,0,1:T(8,128)(2,1)S(1)} reshape(bf16[4,1,2,130816]{3,2,0,1:T(2,128)(2,1)} %slice.219) | data formatting | bytes 4186112 | tf_op jit(solution)/shard_map/while/body/eval_jaxpr/reshape | solution.py:26
  237.3 0.7 fusion.89
  238.1 2.8 tile.14
  240.9 4.3 slice.219
  245.3 6.1 %reshape.289 = bf16[4,1,2,256,511]{4,3,2,0,1:T(8,128)(2,1)S(1)} reshape(bf16[4,1,2,130816]{3,2,0,1:T(2,128)(2,1)} %slice.219) | data formatting | bytes 4186112 | tf_op jit(solution)/shard_map/while/body/eval_jaxpr/reshape | solution.py:26
  252.1 0.7 fusion.89
  253.0 2.8 tile.14
  255.8 4.3 slice.219
  260.1 6.1 %reshape.289 = bf16[4,1,2,256,511]{4,3,2,0,1:T(8,128)(2,1)S(1)} reshape(bf16[4,1,2,130816]{3,2,0,1:T(2,128)(2,1)} %slice.219) | data formatting | bytes 4186112 | tf_op jit(solution)/shard_map/while/body/eval_jaxpr/reshape | solution.py:26
  266.4 0.2 fusion.88
  266.7 0.2 fusion.86
  266.9 0.7 fusion.89
  267.8 2.8 tile.14
  270.6 4.3 slice.219
  274.9 6.1 %reshape.289 = bf16[4,1,2,256,511]{4,3,2,0,1:T(8,128)(2,1)S(1)} reshape(bf16[4,1,2,130816]{3,2,0,1:T(2,128)(2,1)} %slice.219) | data formatting | bytes 4186112 | tf_op jit(solution)/shard_map/while/body/eval_jaxpr/reshape | solution.py:26
  281.2 0.2 fusion.88
  281.5 0.2 fusion.86
  281.7 0.7 fusion.89
  282.6 2.8 tile.14
  285.4 4.3 slice.219
  289.7 6.1 %reshape.289 = bf16[4,1,2,256,511]{4,3,2,0,1:T(8,128)(2,1)S(1)} reshape(bf16[4,1,2,130816]{3,2,0,1:T(2,128)(2,1)} %slice.219) | data formatting | bytes 4186112 | tf_op jit(solution)/shard_map/while/body/eval_jaxpr/reshape | solution.py:26
  296.0 0.2 fusion.88
  296.3 0.2 fusion.86
  296.5 0.7 fusion.89
  297.2 1.2 fusion.14
  298.4 111.7 %psum.23 = bf16[16,1024]{1,0:T(8,128)(2,1)S(1)} all-reduce(f32[16,1024]{1,0:T(8,128)S(1)} %pad_maximum_fusion.1), channel_id=1, replica_groups=mesh['grp'=16,'body'=32] {'body'}, use_global_device_ids=true, to_apply=%region_4.5 | all-reduce | flops 16384 | bytes 98304 | tf_op jit(solution)/shard_map/psum | solution.py:84
  410.7 120.6 %all-reduce.2.cloned.1.call-done = f32[32,16,512]{2,1,0:T(8,128)} async-done(((f32[32,16,512]{2,1,0:T(8,128)}), f32[32,16,512]{2,1,0:T(8,128)}) %all-reduce.2.cloned.1.call-update) | async-done | bytes 1048592 | tf_op jit(solution)/shard_map/psum | solution.py:67
  531.4 1.4 maximum_add_fusion
  (71 shorter events, 6.8 us)
Async XLA Ops:
  6.5 171.3 %copy-start = (bf16[225,2,512]{2,1,0:T(2,128)(2,1)S(1)}, bf16[225,2,512]{2,1,0:T(2,128)(2,1)}, u32[]{:S(2)}) copy-start(bf16[225,2,512]{2,1,0:T(2,128)(2,1)} %param.14) | copy-start | bytes 1382404
  6.5 166.3 %copy-start.2 = (bf16[1,16,2,16,512]{4,3,2,1,0:T(8,128)(2,1)S(1)}, bf16[1,16,2,16,512]{4,3,2,1,0:T(8,128)(2,1)}, u32[]{:S(2)}) copy-start(bf16[1,16,2,16,512]{4,3,2,1,0:T(8,128)(2,1)} %param.19) | copy-start | bytes 1572868
  7.9 168.5 %all-to-all-start = ((s32[32,1,32]{2,1,0:T(1,128)}), s32[32,1,32]{2,1,0:T(1,128)S(1)}, u32[]{:S(2)}, u32[]{:S(2)}) async-start(s32[32,1,32]{2,1,0:T(1,128)} %stack.2), calls=%async_computation | async-start | bytes 32768 | tf_op jit(solution)/shard_map/all_to_all | solution.py:50
  18.5 512.9 %all-reduce.2.cloned.1.call-start = ((), (), s32[]{:S(2)}) async-start(), calls=%async_computation.1 | async-start | bytes 2097152 | tf_op jit(solution)/shard_map/psum | solution.py:67
  22.8 151.0 %copy-start.5 = (s32[32]{0:T(128)S(1)}, s32[32]{0:T(128)}, u32[]{:S(2)}) copy-start(s32[32]{0:T(128)} %param.16) | copy-start | bytes 388
  172.8 1.0 copy-start.3
  178.7 231.4 %copy-start.1 = (bf16[1,2,512,256]{3,2,1,0:T(8,128)(2,1)S(1)}, bf16[1,2,512,256]{3,2,1,0:T(8,128)(2,1)}, u32[]{:S(2)}) copy-start(bf16[1,2,512,256]{3,2,1,0:T(8,128)(2,1)} %param.18) | copy-start | bytes 1572868
  297.2 234.2 %copy-start.4 = (f32[1,16,512]{2,1,0:T(8,128)S(1)}, f32[1,16,512]{2,1,0:T(8,128)}, u32[]{:S(2)}) copy-start(f32[1,16,512]{2,1,0:T(8,128)} %param.12) | copy-start | bytes 98308
Sparse Core Ops, SparseCore 0:
  297.3 233.9 all-reduce.1
